TPU v7x, 32 devices: a whole 2x2x4 slice. The times are simulated.
32 devices in a mesh: grp: 2 (over y), row: 4 (over z), head: 4 (over x, core).
Axes of the slice: x: 2, y: 2, z: 4, core: 2. Of those that a mesh axis runs over, the one named last changes fastest.
Arguments:
- prefill_kv: bfloat16 [1024, 8, 2, 8, 128], P(('grp', 'row'), None, None, 'head'), parts along dimension 0, may hold values from -6 to 6
- page_table: int32 [1024], P(('grp', 'row')), parts along dimension 0, may hold values from 0 to 511, as said below
- prompt_lengths: int32 [16], P('grp'), parts along dimension 0, may hold values from 1 to 128, 512 in all
- prompt_query: bfloat16 [16, 64, 128], P('grp', 'head'), parts along dimension 0, may hold values from -200 to 200
- prompt_new: bfloat16 [16, 2, 8, 128], P('grp', None, 'head'), parts along dimension 0, may hold values from -6 to 6
- decode_query: bfloat16 [16, 64, 128], P(('grp', 'row'), 'head'), parts along dimension 0, may hold values from -200 to 200
- decode_new: bfloat16 [16, 2, 8, 128], P(('grp', 'row'), None, 'head'), parts along dimension 0, may hold values from -6 to 6
- decode_cache: bfloat16 [16, 256, 2, 8, 128], P(('grp', 'row'), None, None, 'head'), parts along dimension 0, may hold values from -6 to 6
- cached_lengths: int32 [16], P(('grp', 'row')), parts along dimension 0, may hold values from 1 to 256, as said below
Outputs:
- decode_out: bfloat16 [16, 8192], P(('grp', 'row'), 'head'), parts along dimension 0
- prompt_out: bfloat16 [16, 8192], P('grp', 'head'), parts along dimension 0
- kv_pool: bfloat16 [1024, 8, 2, 8, 128], P(('grp', 'row'), None, None, 'head'), parts along dimension 0
There are 2 independent parts, one for each index of `grp`. A program takes and returns all parts, laid end to end along the dimension named above; each array names one. Nothing has to cross between parts.
Inputs may be any that keep to these rules, and one draw needn't show every extreme that they name: `page_table`: entries are distinct and cover every pool slot. For a page on device s of row (p // 128 = s), the entry e satisfies (e % 128) // 32 = s: a page goes to device e // 128, into one of the 32 slots that this device keeps for s, so every device sends exactly 32 pages to every device. `prompt_lengths`: the lengths sum to 512; one prompt has exactly 128 pages. `cached_lengths`: some decode sequence uses all 256 positions.
All inputs are finite; a program needn't handle non-finite values.
Results may differ from a plain program's by a relative error of at most 0.0035.
Values may be sent and summed in bfloat16 or wider, within the bound.
A program may use at most 64 MiB of HBM per device.

v0:
```python
import math

import jax
import jax.numpy as jnp
from jax import lax
from jax.sharding import PartitionSpec as P

LOWEST = -1e30


def merged(shard, axis, combine):
    everything = jax.tree.map(lambda part: lax.all_gather(part, axis), shard)
    leading = jax.tree.map(lambda part: part[0], everything)

    def turn(k, so_far):
        return combine(so_far, jax.tree.map(lambda part: part[k], everything))

    return lax.fori_loop(1, lax.axis_size(axis), turn, leading)


def owners_of(prompt_lengths, first_page, page_count):
    end_pages = jnp.cumsum(prompt_lengths)
    page_ids = first_page + jnp.arange(page_count, dtype=jnp.int32)
    return jnp.sum((page_ids[:, None] >= end_pages[None, :]).astype(jnp.int32), axis=1)


def prompt_partial(grouped, pages, page_owner, scaling):
    page_count, page_width = (pages.shape[0], pages.shape[1])
    head_count, head_depth = (pages.shape[3], pages.shape[4])
    key_rows = pages[:, :, 0].reshape(page_count * page_width, head_count, head_depth)
    value_rows = pages[:, :, 1].reshape(page_count * page_width, head_count, head_depth)
    scores = (
        jnp.einsum("jkgd,tkd->jkgt", grouped, key_rows, preferred_element_type=jnp.float32)
        * scaling
    )
    token_owner = jnp.repeat(page_owner, page_width)
    prompt_ids = jnp.arange(grouped.shape[0], dtype=jnp.int32)
    is_live = (token_owner[None, :] == prompt_ids[:, None])[:, None, None, :]
    peak_score = jnp.max(jnp.where(is_live, scores, LOWEST), axis=-1)
    weights = jnp.where(is_live, jnp.exp(scores - peak_score[..., None]), 0.0)
    weight_total = jnp.sum(weights, axis=-1)
    accumulated = jnp.einsum(
        "jkgt,tkd->jkgd",
        weights.astype(jnp.bfloat16),
        value_rows,
        preferred_element_type=jnp.float32,
    )
    return (peak_score, weight_total, accumulated)


def cache_partial(grouped, decode_cache, cached_lengths, scaling):
    scores = (
        jnp.einsum(
            "skgd,stkd->skgt", grouped, decode_cache[:, :, 0], preferred_element_type=jnp.float32
        )
        * scaling
    )
    positions = jnp.arange(decode_cache.shape[1], dtype=jnp.int32)
    is_live = (positions[None, :] < cached_lengths[:, None])[:, None, None, :]
    peak_score = jnp.max(jnp.where(is_live, scores, LOWEST), axis=-1)
    weights = jnp.where(is_live, jnp.exp(scores - peak_score[..., None]), 0.0)
    weight_total = jnp.sum(weights, axis=-1)
    accumulated = jnp.einsum(
        "skgt,stkd->skgd",
        weights.astype(jnp.bfloat16),
        decode_cache[:, :, 1],
        preferred_element_type=jnp.float32,
    )
    return (peak_score, weight_total, accumulated)


def finish(peak_score, weight_total, accumulated, grouped, own_new, scaling):
    own_score = (
        jnp.einsum("jkgd,jkd->jkg", grouped, own_new[:, 0], preferred_element_type=jnp.float32)
        * scaling
    )
    top_score = jnp.maximum(peak_score, own_score)
    rescale = jnp.exp(peak_score - top_score)
    own_weight = jnp.exp(own_score - top_score)
    own_rounded = lax.optimization_barrier(own_weight.astype(jnp.bfloat16)).astype(jnp.float32)
    own_value = own_new[:, 1].astype(jnp.float32)
    numerator = accumulated * rescale[..., None] + own_rounded[..., None] * own_value[:, :, None, :]
    denominator = weight_total * rescale + own_weight
    return (numerator / denominator[..., None]).reshape(grouped.shape[0], -1).astype(jnp.bfloat16)


def join(first_part, second_part):
    peak_first, total_first, accum_first = first_part
    peak_second, total_second, accum_second = second_part
    top_score = jnp.maximum(peak_first, peak_second)
    scale_first = jnp.exp(peak_first - top_score)
    scale_second = jnp.exp(peak_second - top_score)
    weight_total = total_first * scale_first + total_second * scale_second
    accumulated = accum_first * scale_first[..., None] + accum_second * scale_second[..., None]
    return (top_score, weight_total, accumulated)


def per_device(
    prefill_kv,
    page_table,
    prompt_lengths,
    prompt_query,
    prompt_new,
    decode_query,
    decode_new,
    decode_cache,
    cached_lengths,
):
    row_count = lax.axis_size("row")
    row_place = lax.axis_index("row")
    page_count = prefill_kv.shape[0]
    head_count, head_depth = (prefill_kv.shape[3], prefill_kv.shape[4])
    scaling = 1.0 / math.sqrt(head_depth)
    per_pair = page_count // row_count
    page_owner = owners_of(prompt_lengths, row_place * page_count, page_count)
    local_slot = page_table % page_count
    target_slot = page_table // page_count * per_pair + local_slot % per_pair
    sectioned_pages = (
        jnp.zeros((page_count,) + prefill_kv.shape[1:], jnp.bfloat16)
        .at[target_slot]
        .set(prefill_kv)
    )
    grouped = prompt_query.reshape(prompt_query.shape[0], head_count, -1, head_depth)
    decode_grouped = decode_query.reshape(decode_query.shape[0], head_count, -1, head_depth)
    cache_peak, cache_total, cache_accum = cache_partial(
        decode_grouped, decode_cache, cached_lengths, scaling
    )
    decode_out = finish(cache_peak, cache_total, cache_accum, decode_grouped, decode_new, scaling)
    peak_score, weight_total, accumulated = prompt_partial(grouped, prefill_kv, page_owner, scaling)
    kv_pool = lax.all_to_all(sectioned_pages, "row", split_axis=0, concat_axis=0, tiled=True)
    peak_score, weight_total, accumulated = merged(
        (peak_score, weight_total, accumulated), "row", join
    )
    prompt_out = finish(peak_score, weight_total, accumulated, grouped, prompt_new, scaling)
    return (decode_out, prompt_out, kv_pool)


def solution(mesh):
    in_specs = (
        P(("grp", "row"), None, None, "head", None),
        P(("grp", "row")),
        P("grp"),
        P("grp", "head", None),
        P("grp", None, "head", None),
        P(("grp", "row"), "head", None),
        P(("grp", "row"), None, "head", None),
        P(("grp", "row"), None, None, "head", None),
        P(("grp", "row")),
    )
    out_specs = (
        P(("grp", "row"), "head"),
        P("grp", "head"),
        P(("grp", "row"), None, None, "head", None),
    )
    return jax.shard_map(
        per_device, mesh=mesh, in_specs=in_specs, out_specs=out_specs, check_vma=False
    )
```

profile of v0, /device:TPU:0, one launch (start us, length us, event | category | flops | bytes accessed | tf_op | source)
XLA Modules:
  0.0 85.9 jit_solution(13365130478551197415)
XLA Ops:
  0.6 0.7 compare_select_fusion
  1.3 1.4 %copy.60 = bf16[128,8,2,2,128]{4,1,3,2,0:T(8,128)(2,1)S(1)} copy(bf16[128,8,2,2,128]{4,3,2,1,0:T(2,128)(2,1)} %param.11) | data formatting | bytes 2097152 | tf_op args[0]
  2.7 1.1 %broadcast_in_dim.75 = bf16[128,8,2,2,128]{4,1,3,2,0:T(8,128)(2,1)} broadcast(bf16[]{:T(256)} %constant.93.clone.1), dimensions={} | broadcast | bytes 1048578 | tf_op jit(solution)/shard_map/broadcast_in_dim | solution.py:119
  3.8 13.7 %scatter_fusion = bf16[128,8,2,2,128]{4,1,3,2,0:T(8,128)(2,1)} fusion(bf16[128,8,2,2,128]{4,1,3,2,0:T(8,128)(2,1)} %broadcast_in_dim.75, s32[128]{0:T(128)S(1)} %compare_select_fusion, bf16[128,8,2,2,128]{4,1,3,2,0:T(8,128)(2,1)S(1)} %copy.60), kind=kCustom, calls=%fused_computation | custom fusion | bytes 3146240 | tf_op jit(solution)/shard_map/scatter | solution.py:121
  17.5 6.4 %all-to-all-start = ((bf16[128,8,2,2,128]{4,1,3,2,0:T(8,128)(2,1)}), bf16[128,8,2,2,128]{4,1,3,2,0:T(8,128)(2,1)S(1)}, u32[]{:S(2)}, u32[]{:S(2)}) async-start(bf16[128,8,2,2,128]{4,1,3,2,0:T(8,128)(2,1)} %scatter_fusion), calls=%async_computation | async-start | bytes 2097152 | tf_op jit(solution)/shard_map/all_to_all | solution.py:130
  24.0 1.5 %fusion.46 = (bf16[128,8,1,2,128]{4,3,2,1,0:T(2,128)(2,1)S(1)}, bf16[128,8,1,2,128]{4,3,2,1,0:T(2,128)(2,1)}) fusion(bf16[128,8,2,2,128]{4,3,2,1,0:T(2,128)(2,1)S(1)} %copy-done.1), kind=kLoop, calls=%fused_computation.86 | loop fusion | bytes 2097152 | tf_op jit(solution)/shard_map/slice | solution.py:31
  25.5 0.2 reduce-window.8
  25.8 0.4 copy-done.6
  26.2 0.1 convert_reduce_fusion
  26.3 0.1 broadcast_in_dim.71
  26.4 0.1 eq.22
  26.5 0.4 fusion.47
  26.9 0.3 copy-done.4
  27.2 0.1 fusion.29
  27.3 0.3 select_reduce_fusion.1
  27.6 0.2 fusion.21
  27.8 0.2 fusion.8
  28.0 0.6 copy.122
  28.6 0.1 fusion.32
  28.7 0.4 select_reduce_fusion
  29.1 26.0 %all-gather = f32[32,2,8]{2,0,1:T(8,128)S(1)} all-gather(f32[8,2,8]{2,0,1:T(8,128)S(1)} %get-tuple-element.248), channel_id=2, replica_groups=mesh['grp'=2,'row'=4,'head'=4] {'row'}, dimensions={0}, use_global_device_ids=true | all-gather | bytes 2560 | tf_op jit(solution)/shard_map/all_gather | solution.py:12
  55.2 0.3 fusion.14
  55.4 0.3 convolution_bitcast_fusion
  55.8 13.1 %all-gather.1 = f32[32,2,8]{2,0,1:T(8,128)S(1)} all-gather(f32[8,2,8]{2,0,1:T(8,128)S(1)} %fusion.14), channel_id=3, replica_groups=mesh['grp'=2,'row'=4,'head'=4] {'row'}, dimensions={0}, use_global_device_ids=true | all-gather | bytes 2560 | tf_op jit(solution)/shard_map/all_gather | solution.py:12
  68.9 13.8 %all-gather.2 = f32[32,2,8,128]{3,2,0,1:T(8,128)S(1)} all-gather(f32[8,2,8,128]{3,2,0,1:T(8,128)S(1)} %convolution_bitcast_fusion), channel_id=4, replica_groups=mesh['grp'=2,'row'=4,'head'=4] {'row'}, dimensions={0}, use_global_device_ids=true | all-gather | bytes 327680 | tf_op jit(solution)/shard_map/all_gather | solution.py:12
  82.7 0.6 while.19
  82.8 0.1 fusion.52
  82.9 0.1 fusion.52
  83.1 0.1 fusion.52
  83.3 0.1 fusion.20
  83.5 0.6 copy.121
  84.1 1.8 %copy.61 = bf16[128,8,2,2,128]{4,3,2,1,0:T(2,128)(2,1)} copy(bf16[128,8,2,2,128]{4,1,3,2,0:T(8,128)(2,1)S(1)} %all-to-all-done) | data formatting | bytes 2097152
  (41 shorter events, 0.3 us)
Async XLA Ops:
  0.6 28.0 %copy-start = (bf16[8,16,128]{2,1,0:T(8,128)(2,1)S(1)}, bf16[8,16,128]{2,1,0:T(8,128)(2,1)}, u32[]{:S(2)}) copy-start(bf16[8,16,128]{2,1,0:T(8,128)(2,1)} %param.14) | copy-start | bytes 98308
  17.5 6.5 %copy-start.1 = (bf16[128,8,2,2,128]{4,3,2,1,0:T(2,128)(2,1)S(1)}, bf16[128,8,2,2,128]{4,3,2,1,0:T(2,128)(2,1)}, u32[]{:S(2)}) copy-start(bf16[128,8,2,2,128]{4,3,2,1,0:T(2,128)(2,1)} %param.11) | copy-start | bytes 3145732
  17.5 66.6 %all-to-all-start = ((bf16[128,8,2,2,128]{4,1,3,2,0:T(8,128)(2,1)}), bf16[128,8,2,2,128]{4,1,3,2,0:T(8,128)(2,1)S(1)}, u32[]{:S(2)}, u32[]{:S(2)}) async-start(bf16[128,8,2,2,128]{4,1,3,2,0:T(8,128)(2,1)} %scatter_fusion), calls=%async_computation | async-start | bytes 2097152 | tf_op jit(solution)/shard_map/all_to_all | solution.py:130
  24.0 1.5 %copy-start.7 = (s32[8]{0:T(128)S(1)}, s32[8]{0:T(128)}, u32[]{:S(2)}) copy-start(s32[8]{0:T(128)} %param.13) | copy-start | bytes 100
  24.0 1.7 %copy-start.8 = (s32[2]{0:T(128)S(1)}, s32[2]{0:T(128)}, u32[]{:S(2)}) copy-start(s32[2]{0:T(128)} %param.19) | copy-start | bytes 28
  24.0 2.5 %copy-start.2 = (bf16[2,256,2,2,128]{4,3,2,1,0:T(2,128)(2,1)S(1)}, bf16[2,256,2,2,128]{4,3,2,1,0:T(2,128)(2,1)}, u32[]{:S(2)}) copy-start(bf16[2,256,2,2,128]{4,3,2,1,0:T(2,128)(2,1)} %param.18) | copy-start | bytes 1572868
  25.5 0.7 copy-start.5
  25.5 0.7 copy-start.6
  26.5 0.7 copy-start.4
  26.9 1.9 %copy-start.3 = (bf16[128,8,1,2,128]{4,3,2,1,0:T(2,128)(2,1)S(1)}, bf16[128,8,1,2,128]{4,3,2,1,0:T(2,128)(2,1)}, u32[]{:S(2)}) copy-start(bf16[128,8,1,2,128]{4,3,2,1,0:T(2,128)(2,1)} %get-tuple-element.235) | copy-start | bytes 1572868
where the time goes:
time: 86.7 us; the launch traced here: 85.9 us
  blocking collectives  52.9 us (61%)
  local copies, waits for them, and re-layouts  22.1 us (25%)
  starting transfers between devices  6.45 us (7%)
  other arithmetic  2.03 us (2%)
  matrix products  1.41 us (2%)
    all_gather x3, blocking collectives, merged(): everything = jax.tree.map(lambda part: lax.all_gather(part, axis), shard)  52.9 us
    scatter x1, local copies, waits for them, and re-layouts, per_device(): sectioned_pages = jnp.zeros((page_count,) + prefill_kv.shape[1:], jnp.bfl...  13.7 us
    all_to_all x1, starting transfers between devices, per_device(): lax.all_to_all(sectioned_pages, 'row', split_axis=0, concat_axis=0, tiled...  6.45 us
    unnamed x22, local copies, waits for them, and re-layouts  5.23 us
  transfers between devices with their start and end apart: 1, of which 0 were waited for; matrix products, arithmetic and copies ran while one was open for 7% of the time, Pallas kernels for 0%

commit v1 on v0

v1 whole, which is shorter than its diff:
```python
import functools
import math

import jax
import jax.numpy as jnp
from jax import lax
from jax.experimental import pallas as pl
from jax.experimental.pallas import tpu as pltpu
from jax.sharding import PartitionSpec as P

MESH = pl.DeviceIdType.MESH
LOWEST = -1e30
FLOOR = -1e29
LANES = 128
CONTRACT_LAST = (((1,), (1,)), ((), ()))


def partner(me, count, step):
    if count & (count - 1):
        return lax.rem(me + step, count)
    place, bit = 0, 1
    while bit < count:
        here = (me // bit) % 2
        place = place + bit * ((1 - here) if step & bit else here)
        bit *= 2
    return place


def softmax_pass(query, blocks, scores_ref, scaling):
    rows = query.shape[0]
    lane = lax.broadcasted_iota(jnp.int32, (rows, LANES), 1)
    peak = jnp.full((rows, LANES), FLOOR, jnp.float32)
    for load, width, at, first, lo, hi in blocks:
        raw = lax.dot_general(query, load(), CONTRACT_LAST, preferred_element_type=jnp.float32)
        for part in range(width // LANES):
            column = lane + (first + part * LANES)
            live = (column >= lo) & (column < hi)
            here = raw[:, part * LANES : (part + 1) * LANES] * scaling
            here = jnp.where(live, here, LOWEST)
            scores_ref[:, pl.ds(at + part * LANES, LANES)] = here
            peak = jnp.maximum(peak, here)
    top = jnp.max(peak, axis=1, keepdims=True)
    total = jnp.zeros((rows, LANES), jnp.float32)
    accumulated = jnp.zeros((rows, LANES), jnp.float32)
    for load, width, at, first, lo, hi in blocks:
        parts = []
        for part in range(width // LANES):
            weight = jnp.exp(scores_ref[:, pl.ds(at + part * LANES, LANES)] - top)
            total = total + weight
            parts.append(pltpu.roll(weight, 2, 1).astype(jnp.bfloat16))
        accumulated = accumulated + jnp.dot(
            jnp.concatenate(parts, axis=1), load(), preferred_element_type=jnp.float32
        )
    return top, jnp.sum(total, axis=1, keepdims=True), accumulated


def kernel(
    count,
    scaling,
    source_ref,
    lengths_ref,
    cached_ref,
    pages_hbm,
    cache_hbm,
    query_ref,
    new_ref,
    decode_query_ref,
    decode_new_ref,
    decode_out_ref,
    prompt_out_ref,
    pool_ref,
    pages,
    cache,
    sections,
    own_rows,
    decode_own_rows,
    scores,
    decode_scores,
    staged,
    decode_staged,
    accs,
    stats,
    local_sem,
    send_sem,
    recv_sem,
    acc_send_sem,
    acc_recv_sem,
    stat_send_sem,
    stat_recv_sem,
):
    me = lax.axis_index("row")
    page_count, page_rows = pages.shape[0], pages.shape[1]
    per_pair = page_count // count
    heads = query_ref.shape[1]
    prompts = query_ref.shape[0]
    barrier = pltpu.get_barrier_semaphore()
    for step in range(1, count):
        pl.semaphore_signal(
            barrier, inc=1, device_id={"row": partner(me, count, step)}, device_id_type=MESH
        )
    pages_in = pltpu.make_async_copy(pages_hbm, pages, local_sem.at[0])
    pages_in.start()
    cache_in = pltpu.make_async_copy(cache_hbm, cache, local_sem.at[1])
    cache_in.start()

    def gather(place):
        def body(i, carry):
            slot = place * per_pair + i
            sections[slot] = pages[source_ref[slot]]
            return carry

        lax.fori_loop(0, per_pair, body, 0, unroll=min(8, per_pair))

    pages_in.wait()
    sends = []
    for step in reversed(range(1, count)):
        place = partner(me, count, step)
        gather(place)
        if step == count - 1:
            pl.semaphore_wait(barrier, count - 1)
        send = pltpu.make_async_remote_copy(
            src_ref=sections.at[pl.ds(place * per_pair, per_pair)],
            dst_ref=pool_ref.at[pl.ds(me * per_pair, per_pair)],
            send_sem=send_sem.at[step - 1],
            recv_sem=recv_sem.at[step - 1],
            device_id={"row": place},
            device_id_type=MESH,
        )
        send.start()
        sends.append(send)
    gather(me)
    kept = pltpu.make_async_copy(
        sections.at[pl.ds(me * per_pair, per_pair)],
        pool_ref.at[pl.ds(me * per_pair, per_pair)],
        local_sem.at[2],
    )
    kept.start()

    rows = prompts * heads
    row = lax.broadcasted_iota(jnp.int32, (rows, LANES), 0)
    lane = lax.broadcasted_iota(jnp.int32, (rows, LANES), 1)
    head_live = lane % 4 == (row // (heads // 2)) % 2
    far = jnp.int32(1 << 30)
    lo = jnp.zeros((rows, LANES), jnp.int32)
    hi = jnp.zeros((rows, LANES), jnp.int32)
    begin = -me * page_count
    for prompt in range(prompts):
        end = begin + lengths_ref[prompt]
        mine = row // heads == prompt
        lo = jnp.where(mine, begin * page_rows, lo)
        hi = jnp.where(mine, end * page_rows, hi)
        begin = end
    lo = jnp.where(head_live, lo, far)
    own_lo = jnp.where(head_live, (row // heads) * 4, far)
    own_hi = (row // heads) * 4 + 4
    own_lo = jnp.where(me == 0, own_lo, far)
    own_rows[...] = jnp.zeros_like(own_rows)
    own_rows[: new_ref.shape[0], :] = new_ref[...]
    query = query_ref[...].reshape(rows, LANES)
    chunk = 32
    blocks = [(lambda: own_rows[...], LANES, page_count * page_rows, 0, own_lo, own_hi)]
    for at in range(0, page_count, chunk):
        blocks.append(
            (
                lambda at=at: pages[at : at + chunk].reshape(chunk * page_rows, LANES),
                chunk * page_rows,
                at * page_rows,
                at * page_rows,
                lo,
                hi,
            )
        )
    top, total, accumulated = softmax_pass(query, blocks, scores, scaling)
    accs[me] = accumulated.astype(jnp.bfloat16)
    eye = row == lane

    def as_row(column):
        return jnp.sum(jnp.where(eye, column, 0.0), axis=0, keepdims=True)

    def as_column(line):
        return jnp.sum(jnp.where(eye, line, 0.0), axis=1, keepdims=True)

    stats[me] = jnp.concatenate(
        [as_row(top), as_row(total), jnp.zeros((6, LANES), jnp.float32)], axis=0
    )
    for step in reversed(range(1, count)):
        place = partner(me, count, step)
        for held, out_sem, in_sem in (
            (accs, acc_send_sem, acc_recv_sem),
            (stats, stat_send_sem, stat_recv_sem),
        ):
            send = pltpu.make_async_remote_copy(
                src_ref=held.at[me],
                dst_ref=held.at[me],
                send_sem=out_sem.at[step - 1],
                recv_sem=in_sem.at[step - 1],
                device_id={"row": place},
                device_id_type=MESH,
            )
            send.start()
            sends.append(send)

    seqs = decode_query_ref.shape[0]
    cache_rows = cache.shape[1]
    cache_in.wait()
    decode_own_rows[...] = jnp.zeros_like(decode_own_rows)
    decode_own_rows[: decode_new_ref.shape[0], :] = decode_new_ref[...].astype(jnp.float32)
    row = lax.broadcasted_iota(jnp.int32, (heads, LANES), 0)
    lane = lax.broadcasted_iota(jnp.int32, (heads, LANES), 1)
    head_live = lane % 4 == (row // (heads // 2)) % 2
    for seq in range(seqs):
        lo = jnp.where(head_live, 0, far)
        hi = jnp.full((heads, LANES), cached_ref[seq] * 4, jnp.int32)
        own_lo = jnp.where(head_live, seq * 4, far)
        own_hi = jnp.full((heads, LANES), seq * 4 + 4, jnp.int32)
        blocks = [
            (
                lambda: decode_own_rows[...].astype(jnp.bfloat16),
                LANES,
                cache_rows,
                0,
                own_lo,
                own_hi,
            ),
            (lambda seq=seq: cache[seq], cache_rows, 0, 0, lo, hi),
        ]
        top, total, accumulated = softmax_pass(
            decode_query_ref[seq], blocks, decode_scores, scaling
        )
        decode_staged[seq * heads : (seq + 1) * heads, :] = accumulated / total
    for head in range(heads):
        decode_out_ref[:, head * LANES : (head + 1) * LANES] = decode_staged[
            pl.ds(head, seqs, stride=heads), :
        ].astype(jnp.bfloat16)

    for send in sends[count - 1 :]:
        send.wait_recv()
    top = jnp.full((1, LANES), FLOOR, jnp.float32)
    for k in range(count):
        top = jnp.maximum(top, stats[k, 0:1, :])
    total = jnp.zeros((1, LANES), jnp.float32)
    for k in range(count):
        total = total + stats[k, 1:2, :] * jnp.exp(stats[k, 0:1, :] - top)
    joined = jnp.zeros((rows, LANES), jnp.float32)
    for k in range(count):
        share = as_column(jnp.exp(stats[k, 0:1, :] - top) / total)
        joined = joined + accs[k].astype(jnp.float32) * share
    staged[...] = joined
    for head in range(heads):
        prompt_out_ref[:, head * LANES : (head + 1) * LANES] = staged[
            pl.ds(head, prompts, stride=heads), :
        ].astype(jnp.bfloat16)

    kept.wait()
    for send in sends[: count - 1]:
        send.wait_recv()
    for send in sends:
        send.wait_send()


def per_device(
    prefill_kv,
    page_table,
    prompt_lengths,
    prompt_query,
    prompt_new,
    decode_query,
    decode_new,
    decode_cache,
    cached_lengths,
):
    count = lax.axis_size("row")
    page_count = prefill_kv.shape[0]
    head_depth = prefill_kv.shape[4]
    page_rows = math.prod(prefill_kv.shape[1:4])
    per_pair = page_count // count
    prompts, heads = prompt_query.shape[:2]
    seqs = decode_query.shape[0]
    cache_rows = math.prod(decode_cache.shape[1:4])
    target = page_table // page_count * per_pair + page_table % per_pair
    ids = jnp.arange(page_count, dtype=jnp.int32)
    source = jnp.sum(jnp.where(target[None, :] == ids[:, None], ids[None, :], 0), axis=1)
    smem = pl.BlockSpec(memory_space=pltpu.SMEM)
    vmem = pl.BlockSpec(memory_space=pltpu.VMEM)
    anywhere = pl.BlockSpec(memory_space=pl.ANY)
    decode_out, prompt_out, pool = pl.pallas_call(
        functools.partial(kernel, count, 1.0 / math.sqrt(head_depth)),
        out_shape=(
            jax.ShapeDtypeStruct((seqs, heads * head_depth), jnp.bfloat16),
            jax.ShapeDtypeStruct((prompts, heads * head_depth), jnp.bfloat16),
            jax.ShapeDtypeStruct((page_count, page_rows, head_depth), jnp.bfloat16),
        ),
        in_specs=[smem] * 3 + [anywhere] * 2 + [vmem] * 4,
        out_specs=(vmem, vmem, anywhere),
        scratch_shapes=[
            pltpu.VMEM((page_count, page_rows, head_depth), jnp.bfloat16),
            pltpu.VMEM((seqs, cache_rows, head_depth), jnp.bfloat16),
            pltpu.VMEM((page_count, page_rows, head_depth), jnp.bfloat16),
            pltpu.VMEM((LANES, head_depth), jnp.bfloat16),
            pltpu.VMEM((LANES, head_depth), jnp.float32),
            pltpu.VMEM((prompts * heads, page_count * page_rows + LANES), jnp.float32),
            pltpu.VMEM((heads, cache_rows + LANES), jnp.float32),
            pltpu.VMEM((prompts * heads, head_depth), jnp.float32),
            pltpu.VMEM((seqs * heads, head_depth), jnp.float32),
            pltpu.VMEM((count, prompts * heads, head_depth), jnp.bfloat16),
            pltpu.VMEM((count, 8, LANES), jnp.float32),
            pltpu.SemaphoreType.DMA((3,)),
            pltpu.SemaphoreType.DMA((count - 1,)),
            pltpu.SemaphoreType.DMA((count - 1,)),
            pltpu.SemaphoreType.DMA((count - 1,)),
            pltpu.SemaphoreType.DMA((count - 1,)),
            pltpu.SemaphoreType.DMA((count - 1,)),
            pltpu.SemaphoreType.DMA((count - 1,)),
        ],
        compiler_params=pltpu.CompilerParams(
            collective_id=0, has_side_effects=True, vmem_limit_bytes=32 * 1024 * 1024
        ),
    )(
        source,
        prompt_lengths,
        cached_lengths,
        prefill_kv.reshape(page_count, page_rows, head_depth),
        decode_cache.reshape(seqs, cache_rows, head_depth),
        prompt_query,
        prompt_new.reshape(-1, head_depth),
        decode_query,
        decode_new.reshape(-1, head_depth),
    )
    return decode_out, prompt_out, pool.reshape(prefill_kv.shape)


def solution(mesh):
    in_specs = (
        P(("grp", "row"), None, None, "head", None),
        P(("grp", "row")),
        P("grp"),
        P("grp", "head", None),
        P("grp", None, "head", None),
        P(("grp", "row"), "head", None),
        P(("grp", "row"), None, "head", None),
        P(("grp", "row"), None, None, "head", None),
        P(("grp", "row")),
    )
    out_specs = (
        P(("grp", "row"), "head"),
        P("grp", "head"),
        P(("grp", "row"), None, None, "head", None),
    )
    return jax.shard_map(
        per_device, mesh=mesh, in_specs=in_specs, out_specs=out_specs, check_vma=False
    )
```

time: 86.7 us -> 40.8 us (0.47)
  blocking collectives: 52.9 us -> 0 us
  Pallas kernels: 0 us -> 32.5 us
  local copies, waits for them, and re-layouts: 22.1 us -> 6.44 us
  starting transfers between devices: 6.45 us -> 0 us
  matrix products: 1.41 us -> 0 us
  other arithmetic: 2.03 us -> 0.78 us
    all_gather x3 -> x0, blocking collectives: 52.9 us -> none  [merged(): everything = jax.tree.map(lambda part: lax.all_gather(part, axis), shard)]
    pallas_call x0 -> x1, Pallas kernels: none -> 32.5 us  [per_device(): pl.pallas_call(functools.partial(kernel, count, 1.0 / math.sqrt(head_dept...]
    scatter x1 -> x0, local copies, waits for them, and re-layouts: 13.7 us -> none  [per_device(): sectioned_pages = jnp.zeros((page_count,) + prefill_kv.shape[1:], jnp.bfl...]
    all_to_all x1 -> x0, starting transfers between devices: 6.45 us -> none  [per_device(): lax.all_to_all(sectioned_pages, 'row', split_axis=0, concat_axis=0, tiled...]
    slice x5 -> x0, local copies, waits for them, and re-layouts: 1.87 us -> none  [the longest x1 1.5 us: prompt_partial(): pages[:, :, 1].reshape(page_count * page_width, head_count, head_depth)]
    dot_general x6 -> x0, matrix products: 1.41 us -> none  [the longest x1 0.4 us: prompt_partial(): jnp.einsum('jkgd,tkd->jkgt', grouped, key_rows, preferred_element_type=jn...]
    unnamed x22 -> x19, local copies, waits for them, and re-layouts: 5.23 us -> 6.44 us
    broadcast_in_dim x2 -> x0, local copies, waits for them, and re-layouts: 1.18 us -> none  [the longest x1 1.11 us: per_device(): jnp.zeros((page_count,) + prefill_kv.shape[1:], jnp.bfloat16)]
  transfers between devices with their start and end apart: 1 -> 0, of which waited for: 0 -> 0; matrix products, arithmetic and copies ran while one was open for 7% -> 0% of each run, Pallas kernels for 0% -> 0%
where the time goes in v1:
time: 40.8 us; the launch traced here: 40.4 us
  Pallas kernels  32.5 us (80%)
  local copies, waits for them, and re-layouts  6.44 us (16%)
  other arithmetic  0.78 us (2%)
  between operations  0.69 us (2%)
    pallas_call x1, Pallas kernels, per_device(): pl.pallas_call(functools.partial(kernel, count, 1.0 / math.sqrt(head_dept...  32.5 us
    unnamed x19, local copies, waits for them, and re-layouts  6.44 us

profile of v1, /device:TPU:0, one launch (start us, length us, event | category | flops | bytes accessed | tf_op | source)
XLA Modules:
  0.0 40.4 jit_solution(11402262153947163439)
XLA Ops:
  0.6 0.0 copy-start.3
  0.6 0.0 copy-start.5
  0.7 0.7 %fusion = s32[128]{0:T(128)S(1)} fusion(s32[128]{0:T(128)} %param.10), kind=kLoop, calls=%fused_computation.8 | loop fusion | flops 3200 | bytes 1024 | tf_op jit(solution)/shard_map/add | solution.py:280
  1.3 0.0 copy-start.6
  1.3 0.0 copy-start.7
  1.3 0.1 select_reduce_fusion.source_ref
  1.5 0.0 copy-done.3
  1.5 0.0 copy-done.5
  1.5 0.5 %copy-done.6 = s32[8]{0:T(128)S(1)} copy-done((s32[8]{0:T(128)S(1)}, s32[8]{0:T(128)}, u32[]{:S(2)}) %copy-start.6) | copy-done | bytes 56
  2.0 0.0 copy-done.7
  2.0 0.0 copy-start
  2.0 1.2 %copy-done = bf16[128,8,2,2,128]{4,3,2,1,0:T(2,128)(2,1)S(1)} copy-done((bf16[128,8,2,2,128]{4,3,2,1,0:T(2,128)(2,1)S(1)}, bf16[128,8,2,2,128]{4,3,2,1,0:T(2,128)(2,1)}, u32[]{:S(2)}) %copy-start) | copy-done | bytes 1048600
  3.2 0.0 copy-start.1
  3.2 1.0 %copy-done.1 = bf16[2,256,2,2,128]{4,3,2,1,0:T(2,128)(2,1)S(1)} copy-done((bf16[2,256,2,2,128]{4,3,2,1,0:T(2,128)(2,1)S(1)}, bf16[2,256,2,2,128]{4,3,2,1,0:T(2,128)(2,1)}, u32[]{:S(2)}) %copy-start.1) | copy-done | bytes 524312
  4.3 0.0 copy-start.2
  4.3 0.8 %copy-done.2 = bf16[8,16,128]{2,1,0:T(8,128)(2,1)S(1)} copy-done((bf16[8,16,128]{2,1,0:T(8,128)(2,1)S(1)}, bf16[8,16,128]{2,1,0:T(8,128)(2,1)}, u32[]{:S(2)}) %copy-start.2) | copy-done | bytes 32792
  5.0 0.0 copy-start.4
  5.0 0.7 %copy-done.4 = bf16[2,16,128]{2,1,0:T(8,128)(2,1)S(1)} copy-done((bf16[2,16,128]{2,1,0:T(8,128)(2,1)S(1)}, bf16[2,16,128]{2,1,0:T(8,128)(2,1)}, u32[]{:S(2)}) %copy-start.4) | copy-done | bytes 8216
  5.7 32.5 %shard_map.112 = (bf16[2,2048]{1,0:T(2,128)(2,1)S(1)}, bf16[8,2048]{1,0:T(8,128)(2,1)S(1)}, bf16[128,32,128]{2,1,0:T(8,128)(2,1)S(1)}) custom-call(s32[128]{0:T(128)S(1)} %select_reduce_fusion.source_ref, s32[8]{0:T(128)S(1)} %copy-done.6, s32[2]{0:T(128)S(1)} %copy-done.7, bf16[128,32,128]{2,1,0:T(8,128)(2,1)S(1)} %bitcast.5, ...), custom_call_target="tpu_custom_call" | custom-call | tf_op jit(solution)/shard_map/pallas_call | solution.py:286
  38.3 0.6 %copy.15 = bf16[2,2048]{1,0:T(2,128)(2,1)} copy(bf16[2,2048]{1,0:T(2,128)(2,1)S(1)} %get-tuple-element.12) | data formatting | bytes 16384
  38.9 0.6 %copy.16 = bf16[8,2048]{1,0:T(8,128)(2,1)} copy(bf16[8,2048]{1,0:T(8,128)(2,1)S(1)} %get-tuple-element.13) | data formatting | bytes 65536
  39.5 1.0 %copy.17 = bf16[128,8,2,2,128]{4,3,2,1,0:T(2,128)(2,1)} copy(bf16[128,8,2,2,128]{4,3,2,1,0:T(2,128)(2,1)S(1)} %bitcast.6) | data formatting | bytes 2097152
Async XLA Ops:
  0.6 0.8 %copy-start.3 = (bf16[8,2,2,128]{3,2,1,0:T(2,128)(2,1)S(1)}, bf16[8,2,2,128]{3,2,1,0:T(2,128)(2,1)}, u32[]{:S(2)}) copy-start(bf16[8,2,2,128]{3,2,1,0:T(2,128)(2,1)} %param.13) | copy-start | bytes 24580
  0.6 0.8 %copy-start.5 = (bf16[2,2,2,128]{3,2,1,0:T(2,128)(2,1)S(1)}, bf16[2,2,2,128]{3,2,1,0:T(2,128)(2,1)}, u32[]{:S(2)}) copy-start(bf16[2,2,2,128]{3,2,1,0:T(2,128)(2,1)} %param.15) | copy-start | bytes 6148
  1.3 0.7 %copy-start.6 = (s32[8]{0:T(128)S(1)}, s32[8]{0:T(128)}, u32[]{:S(2)}) copy-start(s32[8]{0:T(128)} %lengths_ref.1) | copy-start | bytes 100
  1.3 0.7 %copy-start.7 = (s32[2]{0:T(128)S(1)}, s32[2]{0:T(128)}, u32[]{:S(2)}) copy-start(s32[2]{0:T(128)} %cached_ref.1) | copy-start | bytes 28
  2.0 1.2 %copy-start = (bf16[128,8,2,2,128]{4,3,2,1,0:T(2,128)(2,1)S(1)}, bf16[128,8,2,2,128]{4,3,2,1,0:T(2,128)(2,1)}, u32[]{:S(2)}) copy-start(bf16[128,8,2,2,128]{4,3,2,1,0:T(2,128)(2,1)} %param.9) | copy-start | bytes 3145732
  3.2 1.0 %copy-start.1 = (bf16[2,256,2,2,128]{4,3,2,1,0:T(2,128)(2,1)S(1)}, bf16[2,256,2,2,128]{4,3,2,1,0:T(2,128)(2,1)}, u32[]{:S(2)}) copy-start(bf16[2,256,2,2,128]{4,3,2,1,0:T(2,128)(2,1)} %param.16) | copy-start | bytes 1572868
  4.3 0.8 %copy-start.2 = (bf16[8,16,128]{2,1,0:T(8,128)(2,1)S(1)}, bf16[8,16,128]{2,1,0:T(8,128)(2,1)}, u32[]{:S(2)}) copy-start(bf16[8,16,128]{2,1,0:T(8,128)(2,1)} %query_ref.1) | copy-start | bytes 98308
  5.0 0.7 %copy-start.4 = (bf16[2,16,128]{2,1,0:T(8,128)(2,1)S(1)}, bf16[2,16,128]{2,1,0:T(8,128)(2,1)}, u32[]{:S(2)}) copy-start(bf16[2,16,128]{2,1,0:T(8,128)(2,1)} %decode_query_ref.1) | copy-start | bytes 24580

commit v2 on v1

v2 whole, which is shorter than its diff:
```python
import functools
import math

import jax
import jax.numpy as jnp
from jax import lax
from jax.experimental import pallas as pl
from jax.experimental.pallas import tpu as pltpu
from jax.sharding import PartitionSpec as P

MESH = pl.DeviceIdType.MESH
LOWEST = -1e30
FLOOR = -1e29
LANES = 128
CONTRACT_LAST = (((1,), (1,)), ((), ()))


def partner(me, count, step):
    if count & (count - 1):
        return lax.rem(me + step, count)
    place, bit = 0, 1
    while bit < count:
        here = (me // bit) % 2
        place = place + bit * ((1 - here) if step & bit else here)
        bit *= 2
    return place


def softmax_pass(query, blocks, scores_ref, scaling):
    rows = query.shape[0]
    lane = lax.broadcasted_iota(jnp.int32, (rows, LANES), 1)
    peak = jnp.full((rows, LANES), FLOOR, jnp.float32)
    for load, width, at, first, lo, hi in blocks:
        raw = lax.dot_general(query, load(), CONTRACT_LAST, preferred_element_type=jnp.float32)
        for part in range(width // LANES):
            column = lane + (first + part * LANES)
            live = (column >= lo) & (column < hi)
            here = raw[:, part * LANES : (part + 1) * LANES] * scaling
            here = jnp.where(live, here, LOWEST)
            scores_ref[:, pl.ds(at + part * LANES, LANES)] = here
            peak = jnp.maximum(peak, here)
    top = jnp.max(peak, axis=1, keepdims=True)
    total = jnp.zeros((rows, LANES), jnp.float32)
    accumulated = jnp.zeros((rows, LANES), jnp.float32)
    for load, width, at, first, lo, hi in blocks:
        parts = []
        for part in range(width // LANES):
            weight = jnp.exp(scores_ref[:, pl.ds(at + part * LANES, LANES)] - top)
            total = total + weight
            parts.append(pltpu.roll(weight, 2, 1).astype(jnp.bfloat16))
        accumulated = accumulated + jnp.dot(
            jnp.concatenate(parts, axis=1), load(), preferred_element_type=jnp.float32
        )
    return top, jnp.sum(total, axis=1, keepdims=True), accumulated


def plan_phases(count, per_pair):
    pieces = 4 if per_pair % 4 == 0 else 1
    width = per_pair // pieces
    far_steps = [step for step in range(1, count) if step >= count // 2]
    near_steps = [step for step in range(1, count) if step < count // 2]
    far = [(step, piece * width, width) for piece in range(pieces) for step in far_steps]
    near = [(step, piece * width, width) for piece in range(pieces) for step in near_steps]
    f1, f2 = len(far) * 3 // 8, len(far) * 6 // 8
    n1, n2 = len(near) // 4, len(near) * 3 // 4
    return (far[:f1] + near[:n1], far[f1:f2] + near[n1:n2], far[f2:] + near[n2:])


def kernel(
    count,
    scaling,
    source_ref,
    lengths_ref,
    cached_ref,
    pages_hbm,
    cache_hbm,
    query_hbm,
    new_hbm,
    decode_query_hbm,
    decode_new_hbm,
    decode_out_ref,
    prompt_out_ref,
    pool_ref,
    pages,
    cache,
    query,
    new,
    decode_query,
    decode_new,
    sections,
    own_rows,
    decode_own_rows,
    scores,
    decode_scores,
    staged,
    decode_staged,
    outbox,
    inbox,
    gathered,
    local_sem,
    send_sem,
    recv_sem,
    part_send_sem,
    part_recv_sem,
    out_send_sem,
    out_recv_sem,
):
    me = lax.axis_index("row")
    page_count, page_rows = pages.shape[0], pages.shape[1]
    per_pair = page_count // count
    prompts, heads = query.shape[:2]
    rows = prompts * heads
    share = gathered.shape[1]
    split = share != rows
    barrier = pltpu.get_barrier_semaphore()
    for step in range(1, count):
        pl.semaphore_signal(
            barrier, inc=1, device_id={"row": partner(me, count, step)}, device_id_type=MESH
        )
    incoming = [
        pltpu.make_async_copy(there, here, local_sem.at[i])
        for i, (there, here) in enumerate(
            (
                (pages_hbm, pages),
                (query_hbm, query),
                (new_hbm, new),
                (cache_hbm, cache),
                (decode_query_hbm, decode_query),
                (decode_new_hbm, decode_new),
            )
        )
    ]
    for copy in incoming:
        copy.start()

    def gather(place, first, width):
        def body(i, carry):
            slot = place * per_pair + first + i
            sections[slot] = pages[source_ref[slot]]
            return carry

        lax.fori_loop(0, width, body, 0, unroll=min(8, width))

    page_sends = []

    def send_pages(phase):
        for step, first, width in phase:
            place = partner(me, count, step)
            at = len(page_sends)
            send = pltpu.make_async_remote_copy(
                src_ref=sections.at[pl.ds(place * per_pair + first, width)],
                dst_ref=pool_ref.at[pl.ds(me * per_pair + first, width)],
                send_sem=send_sem.at[at],
                recv_sem=recv_sem.at[at],
                device_id={"row": place},
                device_id_type=MESH,
            )
            send.start()
            page_sends.append(send)

    def exchange(source, target, out_sem, in_sem):
        sends = []
        for step in reversed(range(1, count)):
            place = partner(me, count, step)
            send = pltpu.make_async_remote_copy(
                src_ref=source(place),
                dst_ref=target,
                send_sem=out_sem.at[step - 1],
                recv_sem=in_sem.at[step - 1],
                device_id={"row": place},
                device_id_type=MESH,
            )
            send.start()
            sends.append(send)
        return sends

    phases = plan_phases(count, per_pair)
    incoming[0].wait()
    for step, first, width in phases[0]:
        gather(partner(me, count, step), first, width)
    pl.semaphore_wait(barrier, count - 1)
    send_pages(phases[0])
    for step, first, width in phases[1] + phases[2]:
        gather(partner(me, count, step), first, width)
    gather(me, 0, per_pair)
    kept = pltpu.make_async_copy(
        sections.at[pl.ds(me * per_pair, per_pair)],
        pool_ref.at[pl.ds(me * per_pair, per_pair)],
        local_sem.at[6],
    )
    kept.start()

    row = lax.broadcasted_iota(jnp.int32, (rows, LANES), 0)
    lane = lax.broadcasted_iota(jnp.int32, (rows, LANES), 1)
    head_live = lane % 4 == (row // (heads // 2)) % 2
    far = jnp.int32(1 << 30)
    lo = jnp.zeros((rows, LANES), jnp.int32)
    hi = jnp.zeros((rows, LANES), jnp.int32)
    begin = -me * page_count
    for prompt in range(prompts):
        end = begin + lengths_ref[prompt]
        mine = row // heads == prompt
        lo = jnp.where(mine, begin * page_rows, lo)
        hi = jnp.where(mine, end * page_rows, hi)
        begin = end
    lo = jnp.where(head_live, lo, far)
    own_lo = jnp.where(head_live, (row // heads) * 4, far)
    own_hi = (row // heads) * 4 + 4
    own_lo = jnp.where(me == 0, own_lo, far)
    incoming[1].wait()
    incoming[2].wait()
    own_rows[...] = jnp.zeros_like(own_rows)
    own_rows[: new.shape[0], :] = new[...]
    chunk = 32
    blocks = [(lambda: own_rows[...], LANES, page_count * page_rows, 0, own_lo, own_hi)]
    for at in range(0, page_count, chunk):
        blocks.append(
            (
                lambda at=at: pages[at : at + chunk].reshape(chunk * page_rows, LANES),
                chunk * page_rows,
                at * page_rows,
                at * page_rows,
                lo,
                hi,
            )
        )
    top, total, accumulated = softmax_pass(
        query[...].reshape(rows, LANES), blocks, scores, scaling
    )
    eye = row == lane
    stats = jnp.concatenate(
        [
            jnp.sum(jnp.where(eye, top, 0.0), axis=0, keepdims=True),
            jnp.sum(jnp.where(eye, total, 0.0), axis=0, keepdims=True),
            jnp.zeros((6, LANES), jnp.float32),
        ],
        axis=0,
    )
    for k in range(rows // share):
        outbox[k, :share, :] = accumulated[k * share : (k + 1) * share, :]
        outbox[k, share:, :] = stats
    inbox[me] = outbox[me if split else 0]
    part_sends = exchange(
        lambda place: outbox.at[place if split else 0], inbox.at[me], part_send_sem, part_recv_sem
    )
    send_pages(phases[1])

    seqs = decode_query.shape[0]
    cache_rows = cache.shape[1]
    for copy in incoming[3:]:
        copy.wait()
    decode_own_rows[...] = jnp.zeros_like(decode_own_rows)
    for seq in range(seqs):
        for kind in range(2):
            at = seq * 4 + kind * 2
            decode_own_rows[at : at + 2, :] = decode_new[seq, kind].astype(jnp.float32)
    row = lax.broadcasted_iota(jnp.int32, (heads, LANES), 0)
    lane = lax.broadcasted_iota(jnp.int32, (heads, LANES), 1)
    head_live = lane % 4 == (row // (heads // 2)) % 2
    for seq in range(seqs):
        lo = jnp.where(head_live, 0, far)
        hi = jnp.full((heads, LANES), cached_ref[seq] * 4, jnp.int32)
        own_lo = jnp.where(head_live, seq * 4, far)
        own_hi = jnp.full((heads, LANES), seq * 4 + 4, jnp.int32)
        blocks = [
            (
                lambda: decode_own_rows[...].astype(jnp.bfloat16),
                LANES,
                cache_rows,
                0,
                own_lo,
                own_hi,
            ),
            (lambda seq=seq: cache[seq], cache_rows, 0, 0, lo, hi),
        ]
        top, total, accumulated = softmax_pass(decode_query[seq], blocks, decode_scores, scaling)
        decode_staged[seq * heads : (seq + 1) * heads, :] = accumulated / total
    for head in range(heads):
        decode_out_ref[:, head * LANES : (head + 1) * LANES] = decode_staged[
            pl.ds(head, seqs, stride=heads), :
        ].astype(jnp.bfloat16)

    for send in part_sends:
        send.wait_recv()
    base = me * share if split else 0
    row = lax.broadcasted_iota(jnp.int32, (share, LANES), 0)
    lane = lax.broadcasted_iota(jnp.int32, (share, LANES), 1)
    eye = row + base == lane
    top = jnp.full((1, LANES), FLOOR, jnp.float32)
    for k in range(count):
        top = jnp.maximum(top, inbox[k, share : share + 1, :])
    total = jnp.zeros((1, LANES), jnp.float32)
    for k in range(count):
        total = total + inbox[k, share + 1 : share + 2, :] * jnp.exp(
            inbox[k, share : share + 1, :] - top
        )
    joined = jnp.zeros((share, LANES), jnp.float32)
    for k in range(count):
        weight = jnp.exp(inbox[k, share : share + 1, :] - top) / total
        weight = jnp.sum(jnp.where(eye, weight, 0.0), axis=1, keepdims=True)
        joined = joined + inbox[k, :share, :] * weight
    gathered[me if split else 0] = joined.astype(jnp.bfloat16)
    out_sends = []
    if split:
        out_sends = exchange(
            lambda place: gathered.at[me], gathered.at[me], out_send_sem, out_recv_sem
        )
    send_pages(phases[2])
    for send in out_sends:
        send.wait_recv()
    for k in range(rows // share):
        staged[k * share : (k + 1) * share, :] = gathered[k].astype(jnp.float32)
    for head in range(heads):
        prompt_out_ref[:, head * LANES : (head + 1) * LANES] = staged[
            pl.ds(head, prompts, stride=heads), :
        ].astype(jnp.bfloat16)

    kept.wait()
    for send in page_sends:
        send.wait_recv()
    for send in part_sends + out_sends + page_sends:
        send.wait_send()


def write_out(first, second, third, first_out, second_out, third_out, sem):
    copies = [
        pltpu.make_async_copy(here, there, sem.at[i])
        for i, (here, there) in enumerate(
            ((third, third_out), (second, second_out), (first, first_out))
        )
    ]
    for copy in copies:
        copy.start()
    for copy in copies:
        copy.wait()


def per_device(
    prefill_kv,
    page_table,
    prompt_lengths,
    prompt_query,
    prompt_new,
    decode_query,
    decode_new,
    decode_cache,
    cached_lengths,
):
    count = lax.axis_size("row")
    page_count = prefill_kv.shape[0]
    head_depth = prefill_kv.shape[4]
    page_rows = math.prod(prefill_kv.shape[1:4])
    per_pair = page_count // count
    prompts, heads = prompt_query.shape[:2]
    rows = prompts * heads
    share = rows // count if rows % (16 * count) == 0 else rows
    seqs = decode_query.shape[0]
    cache_rows = math.prod(decode_cache.shape[1:4])
    messages = sum(len(phase) for phase in plan_phases(count, per_pair))
    target = page_table // page_count * per_pair + page_table % per_pair
    ids = jnp.arange(page_count, dtype=jnp.int32)
    source = jnp.sum(jnp.where(target[None, :] == ids[:, None], ids[None, :], 0), axis=1)
    smem = pl.BlockSpec(memory_space=pltpu.SMEM)
    vmem = pl.BlockSpec(memory_space=pltpu.VMEM)
    hbm = pl.BlockSpec(memory_space=pltpu.HBM)
    anywhere = pl.BlockSpec(memory_space=pl.ANY)
    bf16, f32 = jnp.bfloat16, jnp.float32
    out_shape = (
        jax.ShapeDtypeStruct((seqs, heads * head_depth), bf16),
        jax.ShapeDtypeStruct((prompts, heads * head_depth), bf16),
        jax.ShapeDtypeStruct((page_count, page_rows, head_depth), bf16),
    )
    vmem_shape = (
        pltpu.VMEM((seqs, heads * head_depth), bf16),
        pltpu.VMEM((prompts, heads * head_depth), bf16),
        pltpu.VMEM((page_count, page_rows, head_depth), bf16),
    )
    results = pl.pallas_call(
        functools.partial(kernel, count, 1.0 / math.sqrt(head_depth)),
        out_shape=vmem_shape,
        in_specs=[smem] * 3 + [hbm] * 6,
        out_specs=(vmem, vmem, vmem),
        scratch_shapes=[
            pltpu.VMEM((page_count, page_rows, head_depth), bf16),
            pltpu.VMEM((seqs, cache_rows, head_depth), bf16),
            pltpu.VMEM(prompt_query.shape, bf16),
            pltpu.VMEM((prompts * 4, head_depth), bf16),
            pltpu.VMEM(decode_query.shape, bf16),
            pltpu.VMEM(decode_new.shape, bf16),
            pltpu.VMEM((page_count, page_rows, head_depth), bf16),
            pltpu.VMEM((LANES, head_depth), bf16),
            pltpu.VMEM((LANES, head_depth), f32),
            pltpu.VMEM((rows, page_count * page_rows + LANES), f32),
            pltpu.VMEM((heads, cache_rows + LANES), f32),
            pltpu.VMEM((rows, head_depth), f32),
            pltpu.VMEM((seqs * heads, head_depth), f32),
            pltpu.VMEM((rows // share, share + 8, LANES), f32),
            pltpu.VMEM((count, share + 8, LANES), f32),
            pltpu.VMEM((rows // share, share, LANES), bf16),
            pltpu.SemaphoreType.DMA((7,)),
            pltpu.SemaphoreType.DMA((messages,)),
            pltpu.SemaphoreType.DMA((messages,)),
            pltpu.SemaphoreType.DMA((count - 1,)),
            pltpu.SemaphoreType.DMA((count - 1,)),
            pltpu.SemaphoreType.DMA((count - 1,)),
            pltpu.SemaphoreType.DMA((count - 1,)),
        ],
        compiler_params=pltpu.CompilerParams(
            collective_id=0, has_side_effects=True, vmem_limit_bytes=58 * 1024 * 1024
        ),
    )(
        source,
        prompt_lengths,
        cached_lengths,
        prefill_kv.reshape(page_count, page_rows, head_depth),
        decode_cache.reshape(seqs, cache_rows, head_depth),
        prompt_query,
        prompt_new.reshape(-1, head_depth),
        decode_query,
        decode_new,
    )
    decode_out, prompt_out, pool = pl.pallas_call(
        write_out,
        out_shape=out_shape,
        in_specs=[vmem] * 3,
        out_specs=(hbm,) * 3,
        scratch_shapes=[pltpu.SemaphoreType.DMA((3,))],
    )(*(pltpu.with_memory_space_constraint(x, pltpu.VMEM) for x in results))
    return decode_out, prompt_out, pool.reshape(prefill_kv.shape)


def solution(mesh):
    in_specs = (
        P(("grp", "row"), None, None, "head", None),
        P(("grp", "row")),
        P("grp"),
        P("grp", "head", None),
        P("grp", None, "head", None),
        P(("grp", "row"), "head", None),
        P(("grp", "row"), None, "head", None),
        P(("grp", "row"), None, None, "head", None),
        P(("grp", "row")),
    )
    out_specs = (
        P(("grp", "row"), "head"),
        P("grp", "head"),
        P(("grp", "row"), None, None, "head", None),
    )
    return jax.shard_map(
        per_device, mesh=mesh, in_specs=in_specs, out_specs=out_specs, check_vma=False
    )
```

time: 40.8 us -> 34.5 us (0.85)
  local copies, waits for them, and re-layouts: 6.44 us -> 0.65 us
    unnamed x19 -> x2, local copies, waits for them, and re-layouts: 6.44 us -> 0.65 us
    pallas_call x1, Pallas kernels: 32.5 us -> 31.4 us  [per_device(): pl.pallas_call(functools.partial(kernel, count, 1.0 / math.sqrt(head_dept...]
    pallas_call x0 -> x1, Pallas kernels: none -> 1 us  [per_device(): pl.pallas_call(write_out, out_shape=out_shape, in_specs=[vmem] * 3, out_s...]
    add x1, other arithmetic: 0.68 us -> 0.01 us  [per_device(): target = page_table // page_count * per_pair + page_table % per_pair]
    reduce_sum x1, other arithmetic: 0.1 us -> 0.63 us  [per_device(): jnp.sum(jnp.where(target[None, :] == ids[:, None], ids[None, :], 0), axis=1)]
where the time goes in v2:
time: 34.5 us; the launch traced here: 34.3 us
  Pallas kernels  32.4 us (94%)
  local copies, waits for them, and re-layouts  0.65 us (2%)
  between operations  0.65 us (2%)
  other arithmetic  0.64 us (2%)
    pallas_call x1, Pallas kernels, per_device(): pl.pallas_call(functools.partial(kernel, count, 1.0 / math.sqrt(head_dept...  31.4 us
    pallas_call x1, Pallas kernels, per_device(): pl.pallas_call(write_out, out_shape=out_shape, in_specs=[vmem] * 3, out_s...  1 us

profile of v2, /device:TPU:0, one launch (start us, length us, event | category | flops | bytes accessed | tf_op | source)
XLA Modules:
  0.0 34.3 jit_solution(14364540418458247539)
XLA Ops:
  0.6 0.0 copy-start
  0.6 0.6 %copy-done = s32[128]{0:T(128)S(1)} copy-done((s32[128]{0:T(128)S(1)}, s32[128]{0:T(128)}, u32[]{:S(2)}) %copy-start) | copy-done | bytes 536
  1.3 0.6 %select_reduce_fusion.source_ref = s32[128]{0:T(128)} fusion(s32[128]{0:T(128)S(1)} %fusion), kind=kLoop, calls=%fused_computation | loop fusion | flops 49024 | bytes 1024 | tf_op jit(solution)/shard_map/reduce_sum | solution.py:362
  1.9 31.4 %shard_map.112 = (bf16[2,2048]{1,0:T(2,128)(2,1)S(1)}, bf16[8,2048]{1,0:T(8,128)(2,1)S(1)}, bf16[128,32,128]{2,1,0:T(8,128)(2,1)S(1)}) custom-call(s32[128]{0:T(128)} %select_reduce_fusion.source_ref, s32[8]{0:T(128)} %lengths_ref.1, s32[2]{0:T(128)} %cached_ref.1, bf16[128,32,128]{2,1,0:T(8,128)(2,1)} %bitcast.4, bf16[2,1024,128]{2,1,0:T(8,128)(2,1)} %bitcast.5, ...), custom_call_target="tpu_custom_call" | custom-call | tf_op jit(solution)/shard_map/pallas_call | solution.py:378
  33.3 1.0 %shard_map.113 = (bf16[2,2048]{1,0:T(2,128)(2,1)}, bf16[8,2048]{1,0:T(8,128)(2,1)}, bf16[128,32,128]{2,1,0:T(8,128)(2,1)}) custom-call(bf16[2,2048]{1,0:T(2,128)(2,1)S(1)} %get-tuple-element.9.first, bf16[8,2048]{1,0:T(8,128)(2,1)S(1)} %get-tuple-element.10.second, bf16[128,32,128]{2,1,0:T(8,128)(2,1)S(1)} %get-tuple-element.11.third), custom_call_target="tpu_custom_call" | custom-call | tf_op jit(solution)/shard_map/pallas_call | solution.py:422
  (1 shorter events, 0.0 us)
Async XLA Ops:
  0.6 0.7 %copy-start = (s32[128]{0:T(128)S(1)}, s32[128]{0:T(128)}, u32[]{:S(2)}) copy-start(s32[128]{0:T(128)} %param.10) | copy-start | bytes 1540

commit v3 on v2

--- a/solution.py
+++ b/solution.py
@@ -69,9 +69,9 @@
 def kernel(
     count,
     scaling,
-    source_ref,
-    lengths_ref,
-    cached_ref,
+    table_hbm,
+    lengths_hbm,
+    cached_hbm,
     pages_hbm,
     cache_hbm,
     query_hbm,
@@ -81,6 +81,11 @@
     decode_out_ref,
     prompt_out_ref,
     pool_ref,
+    table,
+    source,
+    source_ref,
+    lengths_ref,
+    cached_ref,
     pages,
     cache,
     query,
@@ -121,7 +126,10 @@
         pltpu.make_async_copy(there, here, local_sem.at[i])
         for i, (there, here) in enumerate(
             (
+                (table_hbm, table),
                 (pages_hbm, pages),
+                (lengths_hbm, lengths_ref),
+                (cached_hbm, cached_ref),
                 (query_hbm, query),
                 (new_hbm, new),
                 (cache_hbm, cache),
@@ -136,7 +144,7 @@
     def gather(place, first, width):
         def body(i, carry):
             slot = place * per_pair + first + i
-            sections[slot] = pages[source_ref[slot]]
+            sections[slot] = pages[source_ref[0, slot]]
             return carry
 
         lax.fori_loop(0, width, body, 0, unroll=min(8, width))
@@ -176,17 +184,29 @@
 
     phases = plan_phases(count, per_pair)
     incoming[0].wait()
-    for step, first, width in phases[0]:
+    page = lax.broadcasted_iota(jnp.int32, (page_count, page_count), 0)
+    slot = lax.broadcasted_iota(jnp.int32, (page_count, page_count), 1)
+    entry = table[...]
+    target = lax.div(entry, page_count) * per_pair + lax.rem(entry, per_pair)
+    target = jnp.sum(jnp.where(page == slot, target, 0), axis=1, keepdims=True)
+    source[...] = jnp.max(jnp.where(target == slot, page, 0), axis=0, keepdims=True)
+    listed = pltpu.make_async_copy(source, source_ref, local_sem.at[10])
+    listed.start()
+    listed.wait()
+    incoming[1].wait()
+    for at, item in enumerate(phases[0]):
+        step, first, width = item
         gather(partner(me, count, step), first, width)
-    pl.semaphore_wait(barrier, count - 1)
-    send_pages(phases[0])
+        if at == 0:
+            pl.semaphore_wait(barrier, count - 1)
+        send_pages([item])
     for step, first, width in phases[1] + phases[2]:
         gather(partner(me, count, step), first, width)
     gather(me, 0, per_pair)
     kept = pltpu.make_async_copy(
         sections.at[pl.ds(me * per_pair, per_pair)],
         pool_ref.at[pl.ds(me * per_pair, per_pair)],
-        local_sem.at[6],
+        local_sem.at[9],
     )
     kept.start()
 
@@ -196,6 +216,8 @@
     far = jnp.int32(1 << 30)
     lo = jnp.zeros((rows, LANES), jnp.int32)
     hi = jnp.zeros((rows, LANES), jnp.int32)
+    incoming[2].wait()
+    incoming[3].wait()
     begin = -me * page_count
     for prompt in range(prompts):
         end = begin + lengths_ref[prompt]
@@ -207,8 +229,8 @@
     own_lo = jnp.where(head_live, (row // heads) * 4, far)
     own_hi = (row // heads) * 4 + 4
     own_lo = jnp.where(me == 0, own_lo, far)
-    incoming[1].wait()
-    incoming[2].wait()
+    incoming[4].wait()
+    incoming[5].wait()
     own_rows[...] = jnp.zeros_like(own_rows)
     own_rows[: new.shape[0], :] = new[...]
     chunk = 32
@@ -241,13 +263,16 @@
         outbox[k, share:, :] = stats
     inbox[me] = outbox[me if split else 0]
     part_sends = exchange(
-        lambda place: outbox.at[place if split else 0], inbox.at[me], part_send_sem, part_recv_sem
+        lambda place: outbox.at[place if split else 0, pl.ds(0, share + 2)],
+        inbox.at[me, pl.ds(0, share + 2)],
+        part_send_sem,
+        part_recv_sem,
     )
     send_pages(phases[1])
 
     seqs = decode_query.shape[0]
     cache_rows = cache.shape[1]
-    for copy in incoming[3:]:
+    for copy in incoming[6:]:
         copy.wait()
     decode_own_rows[...] = jnp.zeros_like(decode_own_rows)
     for seq in range(seqs):
@@ -357,10 +382,6 @@
     seqs = decode_query.shape[0]
     cache_rows = math.prod(decode_cache.shape[1:4])
     messages = sum(len(phase) for phase in plan_phases(count, per_pair))
-    target = page_table // page_count * per_pair + page_table % per_pair
-    ids = jnp.arange(page_count, dtype=jnp.int32)
-    source = jnp.sum(jnp.where(target[None, :] == ids[:, None], ids[None, :], 0), axis=1)
-    smem = pl.BlockSpec(memory_space=pltpu.SMEM)
     vmem = pl.BlockSpec(memory_space=pltpu.VMEM)
     hbm = pl.BlockSpec(memory_space=pltpu.HBM)
     anywhere = pl.BlockSpec(memory_space=pl.ANY)
@@ -378,9 +399,14 @@
     results = pl.pallas_call(
         functools.partial(kernel, count, 1.0 / math.sqrt(head_depth)),
         out_shape=vmem_shape,
-        in_specs=[smem] * 3 + [hbm] * 6,
+        in_specs=[hbm] * 9,
         out_specs=(vmem, vmem, vmem),
         scratch_shapes=[
+            pltpu.VMEM((1, page_count), jnp.int32),
+            pltpu.VMEM((1, page_count), jnp.int32),
+            pltpu.SMEM((1, page_count), jnp.int32),
+            pltpu.SMEM(prompt_lengths.shape, jnp.int32),
+            pltpu.SMEM(cached_lengths.shape, jnp.int32),
             pltpu.VMEM((page_count, page_rows, head_depth), bf16),
             pltpu.VMEM((seqs, cache_rows, head_depth), bf16),
             pltpu.VMEM(prompt_query.shape, bf16),
@@ -397,7 +423,7 @@
             pltpu.VMEM((rows // share, share + 8, LANES), f32),
             pltpu.VMEM((count, share + 8, LANES), f32),
             pltpu.VMEM((rows // share, share, LANES), bf16),
-            pltpu.SemaphoreType.DMA((7,)),
+            pltpu.SemaphoreType.DMA((11,)),
             pltpu.SemaphoreType.DMA((messages,)),
             pltpu.SemaphoreType.DMA((messages,)),
             pltpu.SemaphoreType.DMA((count - 1,)),
@@ -409,7 +435,7 @@
             collective_id=0, has_side_effects=True, vmem_limit_bytes=58 * 1024 * 1024
         ),
     )(
-        source,
+        page_table.reshape(1, page_count),
         prompt_lengths,
         cached_lengths,
         prefill_kv.reshape(page_count, page_rows, head_depth),

time: 34.5 us -> 32.3 us (0.936)
  Pallas kernels: 32.4 us -> 31.5 us
  local copies, waits for them, and re-layouts: 0.65 us -> 0 us
  other arithmetic: 0.64 us -> 0 us
    pallas_call x1, Pallas kernels: 31.4 us -> 30.5 us  [per_device(): pl.pallas_call(functools.partial(kernel, count, 1.0 / math.sqrt(head_dept...]
    unnamed x2 -> x0, local copies, waits for them, and re-layouts: 0.65 us -> none
    reduce_sum x1 -> x0, other arithmetic: 0.63 us -> none  [per_device(): jnp.sum(jnp.where(target[None, :] == ids[:, None], ids[None, :], 0), axis=1)]
where the time goes in v3:
time: 32.3 us; the launch traced here: 32.2 us
  Pallas kernels  31.5 us (98%)
  between operations  0.64 us (2%)
    pallas_call x1, Pallas kernels, per_device(): pl.pallas_call(functools.partial(kernel, count, 1.0 / math.sqrt(head_dept...  30.5 us
    pallas_call x1, Pallas kernels, per_device(): pl.pallas_call(write_out, out_shape=out_shape, in_specs=[vmem] * 3, out_s...  1 us

profile of v3, /device:TPU:0, one launch (start us, length us, event | category | flops | bytes accessed | tf_op | source)
XLA Modules:
  0.0 32.2 jit_solution(1118651235191182187)
XLA Ops:
  0.6 30.5 %shard_map.112 = (bf16[2,2048]{1,0:T(2,128)(2,1)S(1)}, bf16[8,2048]{1,0:T(8,128)(2,1)S(1)}, bf16[128,32,128]{2,1,0:T(8,128)(2,1)S(1)}) custom-call(s32[1,128]{1,0:T(1,128)} %bitcast.8, s32[8]{0:T(128)} %lengths_hbm.1, s32[2]{0:T(128)} %cached_hbm.1, bf16[128,32,128]{2,1,0:T(8,128)(2,1)} %bitcast.5, bf16[2,1024,128]{2,1,0:T(8,128)(2,1)} %bitcast.6, ...), custom_call_target="tpu_custom_call" | custom-call | tf_op jit(solution)/shard_map/pallas_call | solution.py:399
  31.2 1.0 %shard_map.113 = (bf16[2,2048]{1,0:T(2,128)(2,1)}, bf16[8,2048]{1,0:T(8,128)(2,1)}, bf16[128,32,128]{2,1,0:T(8,128)(2,1)}) custom-call(bf16[2,2048]{1,0:T(2,128)(2,1)S(1)} %get-tuple-element.9.first, bf16[8,2048]{1,0:T(8,128)(2,1)S(1)} %get-tuple-element.10.second, bf16[128,32,128]{2,1,0:T(8,128)(2,1)S(1)} %get-tuple-element.11.third), custom_call_target="tpu_custom_call" | custom-call | tf_op jit(solution)/shard_map/pallas_call | solution.py:448

commit v4 on v3

--- a/solution.py
+++ b/solution.py
@@ -55,14 +55,14 @@
 
 
 def plan_phases(count, per_pair):
-    pieces = 4 if per_pair % 4 == 0 else 1
+    pieces = 2 if per_pair % 2 == 0 else 1
     width = per_pair // pieces
     far_steps = [step for step in range(1, count) if step >= count // 2]
     near_steps = [step for step in range(1, count) if step < count // 2]
     far = [(step, piece * width, width) for piece in range(pieces) for step in far_steps]
     near = [(step, piece * width, width) for piece in range(pieces) for step in near_steps]
-    f1, f2 = len(far) * 3 // 8, len(far) * 6 // 8
-    n1, n2 = len(near) // 4, len(near) * 3 // 4
+    f1, f2 = len(far) * 4 // 8, len(far) * 6 // 8
+    n1, n2 = len(near) * 2 // 4, len(near) * 4 // 4
     return (far[:f1] + near[:n1], far[f1:f2] + near[n1:n2], far[f2:] + near[n2:])
 
 

time: 32.3 us -> 31.3 us (0.969)
  Pallas kernels: 31.5 us -> 30.5 us
    pallas_call x1, Pallas kernels: 30.5 us -> 29.5 us  [per_device(): pl.pallas_call(functools.partial(kernel, count, 1.0 / math.sqrt(head_dept...]
where the time goes in v4:
time: 31.3 us; the launch traced here: 31.1 us
  Pallas kernels  30.5 us (97%)
  between operations  0.64 us (2%)
    pallas_call x1, Pallas kernels, per_device(): pl.pallas_call(functools.partial(kernel, count, 1.0 / math.sqrt(head_dept...  29.5 us
    pallas_call x1, Pallas kernels, per_device(): pl.pallas_call(write_out, out_shape=out_shape, in_specs=[vmem] * 3, out_s...  1 us

profile of v4, /device:TPU:0, one launch (start us, length us, event | category | flops | bytes accessed | tf_op | source)
XLA Modules:
  0.0 31.1 jit_solution(10537513222443502884)
XLA Ops:
  0.6 29.5 %shard_map.112 = (bf16[2,2048]{1,0:T(2,128)(2,1)S(1)}, bf16[8,2048]{1,0:T(8,128)(2,1)S(1)}, bf16[128,32,128]{2,1,0:T(8,128)(2,1)S(1)}) custom-call(s32[1,128]{1,0:T(1,128)} %bitcast.8, s32[8]{0:T(128)} %lengths_hbm.1, s32[2]{0:T(128)} %cached_hbm.1, bf16[128,32,128]{2,1,0:T(8,128)(2,1)} %bitcast.5, bf16[2,1024,128]{2,1,0:T(8,128)(2,1)} %bitcast.6, ...), custom_call_target="tpu_custom_call" | custom-call | tf_op jit(solution)/shard_map/pallas_call | solution.py:399
  30.1 1.0 %shard_map.113 = (bf16[2,2048]{1,0:T(2,128)(2,1)}, bf16[8,2048]{1,0:T(8,128)(2,1)}, bf16[128,32,128]{2,1,0:T(8,128)(2,1)}) custom-call(bf16[2,2048]{1,0:T(2,128)(2,1)S(1)} %get-tuple-element.9.first, bf16[8,2048]{1,0:T(8,128)(2,1)S(1)} %get-tuple-element.10.second, bf16[128,32,128]{2,1,0:T(8,128)(2,1)S(1)} %get-tuple-element.11.third), custom_call_target="tpu_custom_call" | custom-call | tf_op jit(solution)/shard_map/pallas_call | solution.py:448

commit v5 on v4

--- a/solution.py
+++ b/solution.py
@@ -122,12 +122,21 @@
         pl.semaphore_signal(
             barrier, inc=1, device_id={"row": partner(me, count, step)}, device_id_type=MESH
         )
+    quarter = page_count // 4
+
+    def part(ref, i):
+        return ref.at[pl.ds(i * quarter, quarter)]
+
+    later_pages = [
+        pltpu.make_async_copy(part(pages_hbm, i), part(pages, i), local_sem.at[10 + i])
+        for i in range(1, 4)
+    ]
     incoming = [
         pltpu.make_async_copy(there, here, local_sem.at[i])
         for i, (there, here) in enumerate(
             (
                 (table_hbm, table),
-                (pages_hbm, pages),
+                (part(pages_hbm, 0), part(pages, 0)),
                 (lengths_hbm, lengths_ref),
                 (cached_hbm, cached_ref),
                 (query_hbm, query),
@@ -138,7 +147,7 @@
             )
         )
     ]
-    for copy in incoming:
+    for copy in incoming[:2] + later_pages + incoming[2:]:
         copy.start()
 
     def gather(place, first, width):
@@ -193,7 +202,8 @@
     listed = pltpu.make_async_copy(source, source_ref, local_sem.at[10])
     listed.start()
     listed.wait()
-    incoming[1].wait()
+    for copy in incoming[1:2] + later_pages:
+        copy.wait()
     for at, item in enumerate(phases[0]):
         step, first, width = item
         gather(partner(me, count, step), first, width)
@@ -423,7 +433,7 @@
             pltpu.VMEM((rows // share, share + 8, LANES), f32),
             pltpu.VMEM((count, share + 8, LANES), f32),
             pltpu.VMEM((rows // share, share, LANES), bf16),
-            pltpu.SemaphoreType.DMA((11,)),
+            pltpu.SemaphoreType.DMA((14,)),
             pltpu.SemaphoreType.DMA((messages,)),
             pltpu.SemaphoreType.DMA((messages,)),
             pltpu.SemaphoreType.DMA((count - 1,)),

time: 31.3 us -> 31.3 us (level)
  no operation moved by 1% of the time
where the time goes in v5:
time: 31.3 us; the launch traced here: 31.1 us
  Pallas kernels  30.5 us (97%)
  between operations  0.64 us (2%)
    pallas_call x1, Pallas kernels, per_device(): pl.pallas_call(functools.partial(kernel, count, 1.0 / math.sqrt(head_dept...  29.5 us
    pallas_call x1, Pallas kernels, per_device(): pl.pallas_call(write_out, out_shape=out_shape, in_specs=[vmem] * 3, out_s...  1 us

profile of v5, /device:TPU:0, one launch (start us, length us, event | category | flops | bytes accessed | tf_op | source)
XLA Modules:
  0.0 31.1 jit_solution(1693947689292329314)
XLA Ops:
  0.6 29.5 %shard_map.112 = (bf16[2,2048]{1,0:T(2,128)(2,1)S(1)}, bf16[8,2048]{1,0:T(8,128)(2,1)S(1)}, bf16[128,32,128]{2,1,0:T(8,128)(2,1)S(1)}) custom-call(s32[1,128]{1,0:T(1,128)} %bitcast.8, s32[8]{0:T(128)} %lengths_hbm.1, s32[2]{0:T(128)} %cached_hbm.1, bf16[128,32,128]{2,1,0:T(8,128)(2,1)} %bitcast.5, bf16[2,1024,128]{2,1,0:T(8,128)(2,1)} %bitcast.6, ...), custom_call_target="tpu_custom_call" | custom-call | tf_op jit(solution)/shard_map/pallas_call | solution.py:409
  30.1 1.0 %shard_map.113 = (bf16[2,2048]{1,0:T(2,128)(2,1)}, bf16[8,2048]{1,0:T(8,128)(2,1)}, bf16[128,32,128]{2,1,0:T(8,128)(2,1)}) custom-call(bf16[2,2048]{1,0:T(2,128)(2,1)S(1)} %get-tuple-element.9.first, bf16[8,2048]{1,0:T(8,128)(2,1)S(1)} %get-tuple-element.10.second, bf16[128,32,128]{2,1,0:T(8,128)(2,1)S(1)} %get-tuple-element.11.third), custom_call_target="tpu_custom_call" | custom-call | tf_op jit(solution)/shard_map/pallas_call | solution.py:458
